TPU v7x, 256 devices: a whole 4x4x8 slice. The times are simulated.
256 devices in a mesh: frame: 128 (over z, x, y), track: 2 (over core).
Axes of the slice: x: 4, y: 4, z: 8, core: 2. Of those that a mesh axis runs over, the one named last changes fastest.
Arguments:
- feature_maps: bfloat16 [256, 4096, 256], P('frame'), may hold values from -16 to 16
- query_frame: int32 [1024], P('track'), may hold values from 0 to 255
- query_pixel: int32 [2, 1024], P(None, 'track'), may hold values from 0 to 63
- conv_kernel: float32 [3, 512], replicated, may hold values from -3 to 3
- norm_gain: float32 [512], replicated, may hold values from 0.5 to 1.5
- w_in: bfloat16 [2048, 512], P('track'), may hold values from -0.25 to 0.25
- w_out: bfloat16 [2048, 256], P('track'), may hold values from -0.125 to 0.125
Outputs:
- coarse_points: float32 [2, 256, 1024], P(None, 'frame', 'track')
- refined_points: float32 [2, 256, 1024], P(None, 'frame', 'track')
All inputs are finite; a program needn't handle non-finite values.
Results may differ from a plain program's by a relative error of at most 0.0035.
The roundings to bfloat16 on the way count: a program that leaves them out, or rounds other values in their place, can miss the bound.
Values may be sent and summed in bfloat16 or wider, within the bound.
A program may use at most 128 MiB of HBM per device.

v0:
```python
import jax
import jax.numpy as jnp
from jax import lax
from jax.sharding import PartitionSpec as P

C = 256
SIDE = 64
KT = 3


def soft_argmax(queries, frame_map):
    scores = jnp.einsum(
        "tc,pc->tp", queries, frame_map, preferred_element_type=jnp.float32
    ) * C ** (-0.5)
    peak = jnp.max(scores, axis=1, keepdims=True)
    expo = jnp.exp(scores - peak)
    weights = expo / jnp.sum(expo, axis=1, keepdims=True)
    grid = weights.reshape(weights.shape[0], SIDE, SIDE)
    centers = (jnp.arange(SIDE, dtype=jnp.float32) + 0.5) * (2.0 / SIDE) - 1.0
    vertical = jnp.sum(jnp.sum(grid, axis=2) * centers, axis=1)
    horizontal = jnp.sum(jnp.sum(grid, axis=1) * centers, axis=1)
    return (weights, vertical, horizontal)


def mix_tracks(padded, queries, inside, conv_kernel, norm_gain, w_in, w_out):
    length = padded.shape[1] - (KT - 1)
    read_part = jnp.zeros((padded.shape[0], length, C), jnp.float32)
    query_part = jnp.zeros((length, C), jnp.float32)
    for tap_index in range(KT):
        window = padded[:, tap_index : tap_index + length].astype(jnp.float32)
        read_part = read_part + conv_kernel[tap_index, :C] * window
        query_part = (
            query_part
            + conv_kernel[tap_index, C:] * inside[tap_index : tap_index + length][:, None]
        )
    query_part = query_part[None] * queries[:, None, :].astype(jnp.float32)
    blended = jnp.concatenate([read_part, query_part], axis=-1).reshape(-1, 2 * C)
    normed = (
        blended * lax.rsqrt(jnp.mean(blended * blended, axis=1, keepdims=True) + 1e-06) * norm_gain
    ).astype(jnp.bfloat16)
    hidden = jnp.einsum(
        "rm,hm->rh",
        normed,
        lax.all_gather(w_in, "track", axis=0, tiled=True),
        preferred_element_type=jnp.float32,
    )
    hidden = jax.nn.gelu(hidden).astype(jnp.bfloat16)
    update = jnp.dot(
        hidden,
        lax.all_gather(w_out, "track", axis=0, tiled=True),
        preferred_element_type=jnp.float32,
    )
    result = (blended[:, :C] + update).astype(jnp.bfloat16)
    return result.reshape(padded.shape[0], length, C)


def local(feature_maps, query_frame, query_pixel, conv_kernel, norm_gain, w_in, w_out):
    frames_here = feature_maps.shape[0]
    frame_count = frames_here * lax.axis_size("frame")
    first_frame = lax.axis_index("frame") * frames_here
    flat_maps = feature_maps.reshape(-1, C)
    offset_frame = query_frame - first_frame
    owned = (offset_frame >= 0) & (offset_frame < frames_here)
    flat_rows = (
        jnp.clip(offset_frame, 0, frames_here - 1) * (SIDE * SIDE)
        + query_pixel[0] * SIDE
        + query_pixel[1]
    )
    picked = jnp.where(owned[:, None], flat_maps[flat_rows].astype(jnp.float32), 0.0)
    queries = lax.psum(picked, "frame").astype(jnp.bfloat16)
    sampled_list = []
    vertical_list = []
    horizontal_list = []
    for frame_slot in range(frames_here):
        weights, vertical, horizontal = soft_argmax(queries, feature_maps[frame_slot])
        sampled_list.append(
            jnp.dot(
                weights.astype(jnp.bfloat16),
                feature_maps[frame_slot],
                preferred_element_type=jnp.float32,
            ).astype(jnp.bfloat16)
        )
        vertical_list.append(vertical)
        horizontal_list.append(horizontal)
    sampled = jnp.stack(sampled_list, axis=1)
    coarse_points = jnp.stack([jnp.stack(vertical_list, 0), jnp.stack(horizontal_list, 0)], 0)
    half = (KT - 1) // 2
    by_track = lax.all_to_all(sampled, "frame", split_axis=0, concat_axis=1, tiled=True)
    group = by_track.shape[0]
    own_queries = lax.dynamic_slice_in_dim(queries, lax.axis_index("frame") * group, group, 0)
    padded = jnp.pad(by_track, ((0, 0), (half, half), (0, 0)))
    inside = jnp.pad(jnp.ones((frame_count,), jnp.float32), half)
    refined = mix_tracks(padded, own_queries, inside, conv_kernel, norm_gain, w_in, w_out)
    updated = lax.all_to_all(refined, "frame", split_axis=1, concat_axis=0, tiled=True)
    vertical_list = []
    horizontal_list = []
    for frame_slot in range(frames_here):
        weights, vertical, horizontal = soft_argmax(
            updated[:, frame_slot], feature_maps[frame_slot]
        )
        vertical_list.append(vertical)
        horizontal_list.append(horizontal)
    refined_points = jnp.stack([jnp.stack(vertical_list, 0), jnp.stack(horizontal_list, 0)], 0)
    return (coarse_points, refined_points)


def solution(mesh):
    in_specs = (
        P("frame", None, None),
        P("track"),
        P(None, "track"),
        P(),
        P(),
        P("track", None),
        P("track", None),
    )
    out_specs = (P(None, "frame", "track"), P(None, "frame", "track"))
    return jax.shard_map(local, mesh=mesh, in_specs=in_specs, out_specs=out_specs, check_vma=False)
```

profile of v0, /device:TPU:2, one launch (start us, length us, event | category | flops | bytes accessed | tf_op | source)
XLA Modules:
  0.0 867.1 jit_solution(7243862940687633908)
XLA Ops:
  10.8 4.3 gather_fusion
  15.2 681.8 %all-reduce.3 = bf16[512,256]{1,0:T(8,128)(2,1)S(1)} all-reduce(f32[512,256]{1,0:T(8,128)S(1)} %convert_select_fusion), channel_id=1, replica_groups=mesh['frame'=128,'track'=2] {'frame'}, use_global_device_ids=true, to_apply=%region_0.1 | all-reduce | flops 131072 | bytes 786432 | tf_op jit(solution)/shard_map/psum | solution.py:70
  697.1 3.1 multiply_reduce_fusion.2
  700.2 1.4 multiply_reduce_fusion.3
  701.6 1.5 fusion.11
  703.1 1.9 fusion.10
  705.0 3.2 copy-done
  709.5 1.5 fusion.9
  711.0 1.9 fusion.8
  712.9 3.2 copy-done.1
  718.8 16.5 %all-to-all-start = ((bf16[512,2,256]{2,1,0:T(2,128)(2,1)}), bf16[512,2,256]{2,1,0:T(2,128)(2,1)S(1)}, u32[]{:S(2)}, u32[]{:S(2)}) async-start(bf16[512,2,256]{2,1,0:T(2,128)(2,1)} %copy.44), calls=%async_computation | async-start | bytes 1048576 | tf_op jit(solution)/shard_map/all_to_all | solution.py:88
  735.5 15.8 %all-to-all-done = bf16[512,2,256]{2,1,0:T(2,128)(2,1)S(1)} async-done(((bf16[512,2,256]{2,1,0:T(2,128)(2,1)}), bf16[512,2,256]{2,1,0:T(2,128)(2,1)S(1)}, u32[]{:S(2)}, u32[]{:S(2)}) %all-to-all-start) | async-done | bytes 524320 | tf_op jit(solution)/shard_map/all_to_all | solution.py:88
  752.8 2.0 copy.46
  754.8 6.5 fusion.43
  762.6 6.9 all-to-all-start.1
  769.5 9.0 %copy.43 = f32[512,4096]{0,1:T(8,128)} copy(f32[512,4096]{1,0:T(8,128)} %copy-done) | data formatting | bytes 16777216 | tf_op jit(solution)/shard_map/div | solution.py:17
  778.5 9.0 %copy.42 = f32[512,4096]{0,1:T(8,128)} copy(f32[512,4096]{1,0:T(8,128)} %copy-done.1) | data formatting | bytes 16777216 | tf_op jit(solution)/shard_map/div | solution.py:17
  787.5 4.1 reduce_sum.197
  791.6 4.1 reduce_sum.195
  795.7 8.6 bitcast_reduce_fusion.2
  805.5 3.0 multiply_reduce_fusion
  808.5 1.5 fusion.15
  810.0 4.2 fusion.14
  814.1 9.2 %copy.51 = f32[512,4096]{0,1:T(8,128)} copy(f32[512,4096]{1,0:T(8,128)} %fusion.14) | data formatting | bytes 16777216 | tf_op jit(solution)/shard_map/div | solution.py:17
  823.3 4.7 bitcast_reduce_fusion
  828.0 4.1 reduce_sum.208
  832.1 3.0 multiply_reduce_fusion.1
  835.1 1.5 fusion.13
  836.6 4.2 fusion.12
  840.8 9.0 %copy.50 = f32[512,4096]{0,1:T(8,128)} copy(f32[512,4096]{1,0:T(8,128)} %fusion.12) | data formatting | bytes 16777216 | tf_op jit(solution)/shard_map/div | solution.py:17
  849.7 4.7 bitcast_reduce_fusion.1
  854.4 4.1 reduce_sum.206
  (46 shorter events, 13.3 us)
Async XLA Ops:
  7.2 747.6 %all-gather.5.cloned.1.call-start = ((), (), s32[]{:S(2)}) async-start(), calls=%async_computation.3 | async-start | bytes 1572864 | tf_op jit(solution)/shard_map/all_gather | solution.py:50
  7.9 746.9 %all-gather.3.cloned.1.call-start = ((), (), s32[]{:S(2)}) async-start(), calls=%async_computation.2 | async-start | bytes 3145728 | tf_op jit(solution)/shard_map/all_gather | solution.py:44
  697.1 3.1 copy-start.2
  705.0 3.2 copy-start
  712.9 3.2 copy-start.1
  716.1 19.2 %copy-start.3 = (f32[3,512]{1,0:T(4,128)S(1)}, f32[3,512]{1,0:T(4,128)}, u32[]{:S(2)}) copy-start(f32[3,512]{1,0:T(4,128)} %param.10) | copy-start | bytes 18436
  717.4 37.4 %copy-start.4 = (f32[512]{0:T(512)S(1)}, f32[512]{0:T(512)}, u32[]{:S(2)}) copy-start(f32[512]{0:T(512)} %param.11) | copy-start | bytes 6148
  718.8 32.5 %all-to-all-start = ((bf16[512,2,256]{2,1,0:T(2,128)(2,1)}), bf16[512,2,256]{2,1,0:T(2,128)(2,1)S(1)}, u32[]{:S(2)}, u32[]{:S(2)}) async-start(bf16[512,2,256]{2,1,0:T(2,128)(2,1)} %copy.44), calls=%async_computation | async-start | bytes 1048576 | tf_op jit(solution)/shard_map/all_to_all | solution.py:88
  762.6 41.7 %all-to-all-start.1 = ((bf16[4,256,256]{2,0,1:T(4,128)(2,1)}), bf16[4,256,256]{2,0,1:T(4,128)(2,1)S(1)}, u32[]{:S(2)}, u32[]{:S(2)}) async-start(bf16[4,256,256]{2,0,1:T(4,128)(2,1)} %copy.48), calls=%async_computation.1 | async-start | bytes 1048576 | tf_op jit(solution)/shard_map/all_to_all | solution.py:94
Sparse Core Ops, SparseCore 0:
  9.8 17.3 all-gather.4
  28.9 17.1 all-gather.2
where the time goes:
time: 878 us; the launch traced here: 867 us
  blocking collectives  682 us (78%)
  other arithmetic  57.8 us (7%)
  local copies, waits for them, and re-layouts  52.9 us (6%)
  starting transfers between devices  23.4 us (3%)
  matrix products  19.4 us (2%)
  waiting for transfers between devices  17.2 us (2%)
  between operations  14.5 us (2%)
    psum x1, blocking collectives, local(): queries = lax.psum(picked, 'frame').astype(jnp.bfloat16)  682 us
    div x4, local copies, waits for them, and re-layouts, soft_argmax(): weights = expo / jnp.sum(expo, axis=1, keepdims=True)  36.2 us
    reduce_sum x4, other arithmetic, soft_argmax(): vertical = jnp.sum(jnp.sum(grid, axis=2) * centers, axis=1)  18.3 us
  transfers between devices with their start and end apart: 4, of which 1 were waited for; matrix products, arithmetic and copies ran while one was open for 7% of the time, Pallas kernels for 0%

commit v1 on v0

v1 whole, which is shorter than its diff:
```python
import jax
import jax.numpy as jnp
from jax import lax
from jax.sharding import Mesh
from jax.sharding import PartitionSpec as P

C = 256
SIDE = 64
KT = 3
FRAME = ("z", "x", "y")


def soft_argmax(queries, frame_map):
    scores = jnp.einsum(
        "tc,pc->tp", queries, frame_map, preferred_element_type=jnp.float32
    ) * C ** (-0.5)
    peak = jnp.max(scores, axis=1, keepdims=True)
    expo = jnp.exp(scores - peak)
    weights = expo / jnp.sum(expo, axis=1, keepdims=True)
    centers = (jnp.arange(SIDE, dtype=jnp.float32) + 0.5) * (2.0 / SIDE) - 1.0
    rows = jnp.repeat(centers, SIDE)
    columns = jnp.tile(centers, SIDE)
    vertical = jnp.sum(weights * rows, axis=1)
    horizontal = jnp.sum(weights * columns, axis=1)
    return (weights, vertical, horizontal)


def local(feature_maps, query_frame, query_pixel, conv_kernel, norm_gain, w_in, w_out):
    frames_here = feature_maps.shape[0]
    index = lax.axis_index(FRAME)
    count = lax.axis_size(FRAME)
    w_in = lax.all_gather(w_in, "track", axis=0, tiled=True)
    w_out = lax.all_gather(w_out, "track", axis=0, tiled=True)
    flat_maps = feature_maps.reshape(-1, C)
    offset_frame = query_frame - index * frames_here
    owned = (offset_frame >= 0) & (offset_frame < frames_here)
    flat_rows = (
        jnp.clip(offset_frame, 0, frames_here - 1) * (SIDE * SIDE)
        + query_pixel[0] * SIDE
        + query_pixel[1]
    )
    queries = jnp.where(owned[:, None], flat_maps[flat_rows], 0)
    for axis in ("z", "x", "y"):
        queries = lax.psum(queries, axis)
    sampled_list = []
    coarse = []
    for slot in range(frames_here):
        weights, vertical, horizontal = soft_argmax(queries, feature_maps[slot])
        sampled_list.append(
            jnp.dot(
                weights.astype(jnp.bfloat16),
                feature_maps[slot],
                preferred_element_type=jnp.float32,
            ).astype(jnp.bfloat16)
        )
        coarse.append(jnp.stack([vertical, horizontal], 0))
    from_left = lax.ppermute(sampled_list[-1], FRAME, [(i, i + 1) for i in range(count - 1)])
    from_right = lax.ppermute(sampled_list[0], FRAME, [(i + 1, i) for i in range(count - 1)])
    window = [from_left] + sampled_list + [from_right]
    inside = [(index > 0).astype(jnp.float32)] + [1.0] * frames_here
    inside += [(index < count - 1).astype(jnp.float32)]
    refined = []
    for slot in range(frames_here):
        read_part = 0.0
        query_part = 0.0
        for tap in range(KT):
            read_part = read_part + conv_kernel[tap, :C] * window[slot + tap].astype(jnp.float32)
            query_part = query_part + conv_kernel[tap, C:] * inside[slot + tap]
        query_part = query_part * queries.astype(jnp.float32)
        blended = jnp.concatenate([read_part, query_part], axis=-1)
        normed = (
            blended
            * lax.rsqrt(jnp.mean(blended * blended, axis=1, keepdims=True) + 1e-06)
            * norm_gain
        ).astype(jnp.bfloat16)
        hidden = jnp.einsum("rm,hm->rh", normed, w_in, preferred_element_type=jnp.float32)
        hidden = jax.nn.gelu(hidden).astype(jnp.bfloat16)
        update = jnp.dot(hidden, w_out, preferred_element_type=jnp.float32)
        updated = (blended[:, :C] + update).astype(jnp.bfloat16)
        _, vertical, horizontal = soft_argmax(updated, feature_maps[slot])
        refined.append(jnp.stack([vertical, horizontal], 0))
    return (jnp.stack(coarse, 1), jnp.stack(refined, 1))


def solution(mesh):
    sizes = {"y": 4, "x": 4}
    z = mesh.shape["frame"] // 16
    split = Mesh(
        mesh.devices.reshape(z, sizes["x"], sizes["y"], mesh.shape["track"]),
        ("z", "x", "y", "track"),
    )
    in_specs = (
        P(FRAME, None, None),
        P("track"),
        P(None, "track"),
        P(),
        P(),
        P("track", None),
        P("track", None),
    )
    out_specs = (P(None, FRAME, "track"), P(None, FRAME, "track"))
    return jax.shard_map(local, mesh=split, in_specs=in_specs, out_specs=out_specs, check_vma=False)
```

time: 878 us -> 279 us (0.32)
  blocking collectives: 682 us -> 0 us
  waiting for transfers between devices: 17.2 us -> 175 us
  local copies, waits for them, and re-layouts: 52.9 us -> 6.37 us
  other arithmetic: 57.8 us -> 31.5 us
  matrix products: 19.4 us -> 36.3 us
  starting transfers between devices: 23.4 us -> 8.55 us
    psum x1 -> x0, blocking collectives: 682 us -> none  [local(): queries = lax.psum(picked, 'frame').astype(jnp.bfloat16)]
    psum x0 -> x3, waiting for transfers between devices: none -> 171 us  [local(): queries = lax.psum(queries, axis)]
    div x4 -> x0, local copies, waits for them, and re-layouts: 36.2 us -> none  [soft_argmax(): weights = expo / jnp.sum(expo, axis=1, keepdims=True)]
    all_to_all x2 -> x0, starting transfers between devices: 23.4 us -> none  [the longest x1 16.5 us: local(): lax.all_to_all(sampled, 'frame', split_axis=0, concat_axis=1, tiled=True)]
    reduce_sum x9 -> x2, other arithmetic: 35.2 us -> 14 us  [the longest x1 13.8 us: soft_argmax(): vertical = jnp.sum(weights * rows, axis=1)]
    all_to_all x2 -> x0, waiting for transfers between devices: 15.8 us -> none  [the longest x1 15.8 us: local(): lax.all_to_all(sampled, 'frame', split_axis=0, concat_axis=1, tiled=True)]
    dot_general x4, matrix products: 10.4 us -> 23.3 us  [soft_argmax(): jnp.einsum('tc,pc->tp', queries, frame_map, preferred_element_type=jnp.fl...]
    div x4 -> x0, other arithmetic: 12.2 us -> none  [soft_argmax(): weights = expo / jnp.sum(expo, axis=1, keepdims=True)]
  transfers between devices with their start and end apart: 4 -> 7, of which waited for: 1 -> 4; matrix products, arithmetic and copies ran while one was open for 7% -> 7% of each run, Pallas kernels for 0% -> 0%
where the time goes in v1:
time: 279 us; the launch traced here: 273 us
  waiting for transfers between devices  175 us (63%)
  matrix products  36.3 us (13%)
  other arithmetic  31.5 us (11%)
  between operations  15.4 us (6%)
  starting transfers between devices  8.55 us (3%)
  local copies, waits for them, and re-layouts  6.37 us (2%)
    psum x3, waiting for transfers between devices, local(): queries = lax.psum(queries, axis)  171 us
    dot_general x4, matrix products, soft_argmax(): jnp.einsum('tc,pc->tp', queries, frame_map, preferred_element_type=jnp.fl...  23.3 us
    reduce_sum x1, other arithmetic, soft_argmax(): vertical = jnp.sum(weights * rows, axis=1)  13.8 us
    reduce_sum x4, other arithmetic, soft_argmax(): weights = expo / jnp.sum(expo, axis=1, keepdims=True)  13.3 us
    dot_general x2, matrix products, local(): jnp.einsum('rm,hm->rh', normed, w_in, preferred_element_type=jnp.float32)  8.56 us
    ppermute x1, starting transfers between devices, local(): lax.ppermute(sampled_list[0], FRAME, [(i + 1, i) for i in range(count - 1)])  5.87 us
  transfers between devices with their start and end apart: 7, of which 4 were waited for; matrix products, arithmetic and copies ran while one was open for 7% of the time, Pallas kernels for 0%

profile of v1, /device:TPU:2, one launch (start us, length us, event | category | flops | bytes accessed | tf_op | source)
XLA Modules:
  0.0 273.4 jit_solution(8686620003232133565)
XLA Ops:
  8.0 0.8 slice_multiply_fusion
  8.8 0.7 compare_and_fusion
  9.5 0.7 compare_select_fusion
  10.2 4.3 %gather_fusion = bf16[512,256]{1,0:T(8,128)(2,1)S(1)} fusion(bf16[8192,256]{1,0:T(8,128)(2,1)} %bitcast.56, s32[1024]{0:T(1024)S(1)} %pad_clamp_fusion), kind=kCustom, calls=%fused_computation | custom fusion | bytes 526336 | tf_op jit(solution)/shard_map/gather | solution.py:42
  14.6 0.7 broadcast_select_fusion
  15.4 75.6 %all-reduce.4.cloned.1.call-done = bf16[512,256]{0,1:T(8,128)(2,1)} async-done(((bf16[512,256]{0,1:T(8,128)(2,1)}), bf16[512,256]{0,1:T(8,128)(2,1)}) %all-reduce.4.cloned.1.call-update) | async-done | bytes 262160 | tf_op jit(solution)/shard_map/psum | solution.py:44
  91.1 46.5 %all-reduce.6.cloned.1.call-done = bf16[512,256]{0,1:T(8,128)(2,1)} async-done(((bf16[512,256]{0,1:T(8,128)(2,1)}), bf16[512,256]{0,1:T(8,128)(2,1)}) %all-reduce.6.cloned.1.call-update) | async-done | bytes 262160 | tf_op jit(solution)/shard_map/psum | solution.py:44
  137.7 0.5 all-gather.3.cloned.1.call-update
  138.3 0.5 all-gather.5.cloned.1.call-update
  138.8 0.8 multiply_add_fusion
  139.6 48.7 %all-reduce.8.cloned.1.call-done = bf16[512,256]{0,1:T(8,128)(2,1)} async-done(((bf16[512,256]{0,1:T(8,128)(2,1)}), bf16[512,256]{0,1:T(8,128)(2,1)}) %all-reduce.8.cloned.1.call-update) | async-done | bytes 262160 | tf_op jit(solution)/shard_map/psum | solution.py:44
  188.4 3.2 %multiply_reduce_fusion.10 = (f32[512]{0:T(512)S(1)}, f32[512,4096]{1,0:T(8,128)S(1)}) fusion(bf16[512,256]{0,1:T(8,128)(2,1)} %all-reduce.8.cloned.1.call-done, bf16[2,4096,256]{2,1,0:T(8,128)(2,1)} %param.7), kind=kOutput, calls=%fused_computation.15 | convolution fusion | flops 1077935616 | bytes 10749952 | tf_op jit(solution)/shard_map/tc,pc->tp/dot_general | solution.py:14
  191.6 1.5 fusion.3
  193.1 2.2 fusion.54
  195.3 2.5 collective-permute-start
  197.8 1.4 multiply_reduce_fusion.11
  199.2 1.5 fusion.1
  200.7 2.2 fusion.59
  202.9 5.9 %collective-permute-start.1 = (bf16[512,256]{0,1:T(8,128)(2,1)S(1)}, bf16[512,256]{0,1:T(8,128)(2,1)S(1)}, u32[]{:S(2)}, u32[]{:S(2)}) collective-permute-start(bf16[512,256]{0,1:T(8,128)(2,1)S(1)} %fusion.59), channel_id=1, source_target_pairs={{2,0},{4,2},{6,4},{8,6},{10,8},{12,10},{14,12},{16,14},{18,16},{20... | collective-permute-start | bytes 786440 | tf_op jit(solution)/shard_map/ppermute | solution.py:58
  209.2 3.3 %collective-permute-done.1 = bf16[512,256]{0,1:T(8,128)(2,1)S(1)} collective-permute-done((bf16[512,256]{0,1:T(8,128)(2,1)S(1)}, bf16[512,256]{0,1:T(8,128)(2,1)S(1)}, u32[]{:S(2)}, u32[]{:S(2)}) %collective-permute-start.1) | collective-permute-done | bytes 262176 | tf_op jit(solution)/shard_map/ppermute | solution.py:58
  212.5 0.3 fusion.77
  212.8 0.2 multiply_reduce_fusion.12
  213.1 5.0 %fusion.79 = f32[512,2048]{1,0:T(8,128)} fusion(bf16[2048,512]{1,0:T(8,128)(2,1)} %all-gather.3.cloned.1.call-done, f32[512,256]{0,1:T(8,128)S(1)} %get-tuple-element.20, f32[512,256]{0,1:T(8,128)S(1)} %get-tuple-element.18, f32[512]{0:T(512)S(1)} %add_rsqrt_fusion, f32[512]{0:T(512)S(1)} %copy-done.6), kind=kOutput, calls=%fused_computation.88 | convolution fusion | flops 1074790400 | bytes 7344128 | tf_op jit(solution)/shard_map/rm,hm->rh/dot_general | solution.py:76
  218.1 9.4 %multiply_reduce_fusion.8 = (f32[512]{0:T(512)S(1)}, f32[512,4096]{1,0:T(8,128)}) fusion(bf16[2,4096,256]{2,1,0:T(8,128)(2,1)} %param.7, f32[512,256]{0,1:T(8,128)S(1)} %get-tuple-element.18, bf16[2048,256]{1,0:T(8,128)(2,1)} %all-gather.5.cloned.1.call-done, f32[512,2048]{1,0:T(8,128)} %fusion.79), kind=kOutput, calls=%fused_computation.13 | convolution fusion | flops 1624505856 | bytes 16254976 | tf_op jit(solution)/shard_map/tc,pc->tp/dot_general | solution.py:14
  227.5 5.0 %fusion.7 = f32[512]{0:T(512)S(1)} fusion(f32[512,4096]{1,0:T(8,128)} %get-tuple-element.36, f32[512]{0:T(512)S(1)} %get-tuple-element.35), kind=kLoop, calls=%fused_computation.24 | loop fusion | flops 6290944 | bytes 8392704 | tf_op jit(solution)/shard_map/reduce_sum | solution.py:19
  232.5 3.5 %fusion.78 = f32[512,2048]{1,0:T(8,128)} fusion(bf16[2048,512]{1,0:T(8,128)(2,1)S(1)} %copy-done.4, f32[512,256]{0,1:T(8,128)S(1)} %get-tuple-element.21, f32[512,256]{0,1:T(8,128)S(1)} %get-tuple-element.19, f32[512]{0:T(512)S(1)} %copy-done.6, f32[512]{0:T(512)S(1)} %add_rsqrt_fusion.1), kind=kOutput, calls=%fused_computation.87 | convolution fusion | flops 1074790400 | bytes 7344128 | tf_op jit(solution)/shard_map/rm,hm->rh/dot_general | solution.py:76
  236.0 9.3 %multiply_reduce_fusion.9 = (f32[512]{0:T(512)S(1)}, f32[512,4096]{1,0:T(8,128)}) fusion(bf16[2,4096,256]{2,1,0:T(8,128)(2,1)} %param.7, f32[512,256]{0,1:T(8,128)S(1)} %get-tuple-element.19, bf16[2048,256]{1,0:T(8,128)(2,1)} %all-gather.5.cloned.1.call-done, f32[512,2048]{1,0:T(8,128)} %fusion.78), kind=kOutput, calls=%fused_computation.14 | convolution fusion | flops 1624505856 | bytes 16254976 | tf_op jit(solution)/shard_map/tc,pc->tp/dot_general | solution.py:14
  245.4 5.3 %fusion.5 = f32[512]{0:T(512)S(1)} fusion(f32[512,4096]{1,0:T(8,128)} %get-tuple-element.34, f32[512]{0:T(512)S(1)} %get-tuple-element.33), kind=kLoop, calls=%fused_computation.22 | loop fusion | flops 6290944 | bytes 8392704 | tf_op jit(solution)/shard_map/reduce_sum | solution.py:19
  250.7 0.5 copy-done.2
  251.2 13.8 %multiply_reduce_fusion.5 = (f32[512]{0:T(512)S(1)}, f32[512]{0:T(512)S(1)}, f32[512]{0:T(512)S(1)}, f32[512]{0:T(512)S(1)}, f32[512]{0:T(512)S(1)}, /*index=5*/f32[512]{0:T(512)S(1)}, f32[512]{0:T(512)S(1)}, f32[512]{0:T(512)S(1)}) fusion(f32[4096]{0:T(1024)S(1)} %mul.292, f32[4096]{0:T(1024)S(1)} %mul.295, f32[512]{0:T(512)S(1)} %fusion.5, ...), kind=kLoop, calls=%fused_computation.8 | loop fusion | flops 58716160 | bytes 33619968 | tf_op jit(solution)/shard_map/reduce_sum | solution.py:23
  265.0 0.6 copy.12
  265.6 0.6 copy.11
  (40 shorter events, 0.9 us)
Async XLA Ops:
  8.0 83.0 %all-reduce.4.cloned.1.call-start = ((), (), s32[]{:S(2)}) async-start(), calls=%async_computation | async-start | bytes 524288 | tf_op jit(solution)/shard_map/psum | solution.py:44
  15.4 122.2 %all-reduce.6.cloned.1.call-start = ((), (), s32[]{:S(2)}) async-start(), calls=%async_computation.1 | async-start | bytes 524288 | tf_op jit(solution)/shard_map/psum | solution.py:44
  91.0 97.3 %all-reduce.8.cloned.1.call-start = ((), (), s32[]{:S(2)}) async-start(), calls=%async_computation.2 | async-start | bytes 524288 | tf_op jit(solution)/shard_map/psum | solution.py:44
  137.6 75.4 %all-gather.3.cloned.1.call-start = ((), (), s32[]{:S(2)}) async-start(), calls=%async_computation.3 | async-start | bytes 3145728 | tf_op jit(solution)/shard_map/all_gather | solution.py:32
  138.2 79.9 %all-gather.5.cloned.1.call-start = ((), (), s32[]{:S(2)}) async-start(), calls=%async_computation.4 | async-start | bytes 1572864 | tf_op jit(solution)/shard_map/all_gather | solution.py:33
  188.4 4.7 %copy-start.3 = (bf16[2,4096,256]{2,1,0:T(8,128)(2,1)S(1)}, bf16[2,4096,256]{2,1,0:T(8,128)(2,1)}, u32[]{:S(2)}) copy-start(bf16[2,4096,256]{2,1,0:T(8,128)(2,1)} %param.7) | copy-start | bytes 12582916
  191.6 3.7 %copy-start = (f32[512,4096]{1,0:T(8,128)}, f32[512,4096]{1,0:T(8,128)S(1)}, u32[]{:S(2)}) copy-start(f32[512,4096]{1,0:T(8,128)S(1)} %get-tuple-element.30) | copy-start | bytes 25165828
  193.1 4.7 %copy-start.5 = (bf16[512,256]{0,1:T(8,128)(2,1)S(1)}, bf16[512,256]{0,1:T(8,128)(2,1)}, u32[]{:S(2)}) copy-start(bf16[512,256]{0,1:T(8,128)(2,1)} %all-reduce.8.cloned.1.call-done) | copy-start | bytes 786436
  195.3 13.9 %collective-permute-start = (bf16[512,256]{0,1:T(8,128)(2,1)S(1)}, bf16[512,256]{0,1:T(8,128)(2,1)S(1)}, u32[]{:S(2)}, u32[]{:S(2)}) collective-permute-start(bf16[512,256]{0,1:T(8,128)(2,1)S(1)} %fusion.54), channel_id=1, source_target_pairs={{0,2},{2,4},{4,6},{6,8},{8,10},{10,12},{12,14},{14,16},{16,18},{18... | collective-permute-start | bytes 786440 | tf_op jit(solution)/shard_map/ppermute | solution.py:57
  199.2 3.7 %copy-start.1 = (f32[512,4096]{1,0:T(8,128)}, f32[512,4096]{1,0:T(8,128)S(1)}, u32[]{:S(2)}) copy-start(f32[512,4096]{1,0:T(8,128)S(1)} %get-tuple-element.32) | copy-start | bytes 25165828
  200.7 12.4 %copy-start.6 = (f32[512]{0:T(512)S(1)}, f32[512]{0:T(512)}, u32[]{:S(2)}) copy-start(f32[512]{0:T(512)} %param.11) | copy-start | bytes 6148
  202.9 9.5 %collective-permute-start.1 = (bf16[512,256]{0,1:T(8,128)(2,1)S(1)}, bf16[512,256]{0,1:T(8,128)(2,1)S(1)}, u32[]{:S(2)}, u32[]{:S(2)}) collective-permute-start(bf16[512,256]{0,1:T(8,128)(2,1)S(1)} %fusion.59), channel_id=1, source_target_pairs={{2,0},{4,2},{6,4},{8,6},{10,8},{12,10},{14,12},{16,14},{18,16},{20... | collective-permute-start | bytes 786440 | tf_op jit(solution)/shard_map/ppermute | solution.py:58
  227.5 5.0 %copy-start.4 = (bf16[2048,512]{1,0:T(8,128)(2,1)S(1)}, bf16[2048,512]{1,0:T(8,128)(2,1)}, u32[]{:S(2)}) copy-start(bf16[2048,512]{1,0:T(8,128)(2,1)} %all-gather.3.cloned.1.call-done) | copy-start | bytes 6291460
  245.4 5.8 %copy-start.2 = (f32[512,4096]{1,0:T(8,128)S(1)}, f32[512,4096]{1,0:T(8,128)}, u32[]{:S(2)}) copy-start(f32[512,4096]{1,0:T(8,128)} %get-tuple-element.34) | copy-start | bytes 25165828
Sparse Core Ops, SparseCore 0:
  15.5 75.4 all-reduce.3
  93.4 44.1 all-reduce.5
  139.9 48.3 all-reduce.7
Sparse Core Ops, SparseCore 1:
  140.0 17.4 all-gather.2
  159.3 15.5 all-gather.4
